TPU v7x, 32 devices: a whole 2x2x4 slice. The times are simulated.
32 devices in a mesh: grp: 2 (over y), row: 4 (over z), col: 2 (over x), evt: 2 (over core).
Axes of the slice: x: 2, y: 2, z: 4, core: 2. Of those that a mesh axis runs over, the one named last changes fastest.
Arguments:
- sections: float32 [4, 4096], P('evt', ('grp', 'row', 'col')), parts along dimension 1, may hold values from 6.5 to 8.5
- send_list: int32 [8, 2, 4, 64], P(('grp', 'row'), 'col'), parts along dimension 0, may hold values from 0 to 255
- send_count: int32 [8, 2, 4], P(('grp', 'row'), 'col'), parts along dimension 0, may hold values from 32 to 64, as said below
- slot_sender_position: int32 [8, 2, 32], P(('grp', 'row'), 'col'), parts along dimension 0, may hold values from 0 to 255
- block_slot_index: int32 [32, 16], P(('grp', 'row'), 'col'), parts along dimension 0, may hold values from 0 to 31
- hand: float32 [256, 2048], P(('grp', 'row'), 'col'), parts along dimension 0, may hold values from 0.2 to 12
- drain: float32 [256, 2048], P(('grp', 'row'), 'col'), parts along dimension 0, may hold values from 0 to 1.5
- manning: float32 [256, 2048], P(('grp', 'row'), 'col'), parts along dimension 0, may hold values from 0.03 to 0.2
Outputs:
- hand_depth: float32 [4, 256, 2048], P('evt', ('grp', 'row'), 'col'), parts along dimension 1
- final_depth: float32 [4, 256, 2048], P('evt', ('grp', 'row'), 'col'), parts along dimension 1
There are 2 independent parts, one for each index of `grp`. A program takes and returns all parts, laid end to end along the dimension named above; each array names one. Nothing has to cross between parts.
Inputs may be any that keep to these rules, and one draw needn't show every extreme that they name: `send_count`: in every draw some owner's list to some tile row is live in all 64 entries.
All inputs are finite; a program needn't handle non-finite values.
Results may differ from a plain program's by a relative error of at most 0.0002.
Values sent between devices are 32-bit elements; how exact they have to be, the bound alone decides.
A program may use at most 64 MiB of HBM per device.

v0:
```python
import functools

import jax
import jax.numpy as jnp
from jax import lax
from jax.experimental import pallas as pl
from jax.experimental.pallas import tpu as pltpu
from jax.sharding import PartitionSpec as P

STEPS = 16
GRAVITY = 9.81
TIMESTEP = 0.4
SPACING = 10.0
DEPTH_FLOOR = 0.05
DRY_SECTION = -1000.0

VMEM_BYTES = 24 * 1024 * 1024
LANES = 128
SUBLANES = 8
HALO = STEPS
META_ROWS = 8
SSP_ROW = 3
BSI_ROW = 4
SCALE = GRAVITY * TIMESTEP * TIMESTEP / (SPACING * SPACING)
DRAG_SCALE = (
    GRAVITY * TIMESTEP * SCALE ** (7.0 / 3.0) / (SCALE * TIMESTEP / SPACING)
)
REGIONS = tuple(
    (dr, dc) for dr in (-1, 0, 1) for dc in (-1, 0, 1) if (dr, dc) != (0, 0)
)


def row_spans(dr, tile_rows):
    if dr == -1:
        return pl.ds(tile_rows - HALO, HALO), pl.ds(tile_rows + HALO, HALO)
    if dr == 1:
        return pl.ds(0, HALO), pl.ds(tile_rows, HALO)
    return pl.ds(0, tile_rows), pl.ds(0, tile_rows)


def col_spans(dc, tile_cols):
    if dc == -1:
        return pl.ds(tile_cols - LANES, LANES), pl.ds(tile_cols + LANES, LANES)
    if dc == 1:
        return pl.ds(0, LANES), pl.ds(tile_cols, LANES)
    return pl.ds(0, tile_cols), pl.ds(0, tile_cols)


def flood_kernel(
    row_total, col_total,
    sections_in, send_list_in, send_count_in, slot_position_in, block_slot_in, hand, drain, manning,
    hand_depth, final_depth,
    sections, send_list, send_count, slot_position, block_slot, small_sem,
    ext, meta, meta_levels, landed, landed_levels, table, table_levels,
    depth, east, south, bed, top_east, top_south, drag,
    strip_send, strip_recv, meta_send, meta_recv, own_sem, meta_own_sem, table_sem,
):
    r = lax.axis_index("row")
    k = lax.axis_index("col")
    tile_rows, tile_cols = hand.shape
    events, catch_local = sections.shape
    capacity = send_list.shape[3]
    block_rows, block_cols = block_slot.shape
    width = depth.shape[2]
    tiles = depth.shape[1] // SUBLANES
    halo_tiles = HALO // SUBLANES
    own_tiles = tile_rows // SUBLANES
    halves = catch_local // LANES
    terrain = (hand, drain, manning)

    def col_exists(dc):
        return jnp.logical_and(k + dc >= 0, k + dc < col_total)

    def partner(rr, dc):
        if dc == 0:
            return rr != r
        return col_exists(dc)

    barrier = pltpu.get_barrier_semaphore()
    for rr in range(row_total):
        for dc in (-1, 0, 1):
            @pl.when(partner(rr, dc))
            def _():
                pl.semaphore_signal(
                    barrier, inc=1, device_id={"row": rr, "col": k + dc},
                    device_id_type=pl.DeviceIdType.MESH,
                )

    own_copies = [
        pltpu.make_async_copy(
            terrain[array], ext.at[array, pl.ds(0, tile_rows), pl.ds(0, tile_cols)],
            own_sem.at[array],
        )
        for array in range(3)
    ]
    small_copies = [
        pltpu.make_async_copy(source, target, small_sem.at[at])
        for at, (source, target) in enumerate((
            (sections_in, sections), (send_list_in, send_list), (send_count_in, send_count),
            (slot_position_in, slot_position), (block_slot_in, block_slot),
        ))
    ]
    for copy in small_copies + own_copies:
        copy.start()
    for copy in small_copies:
        copy.wait()

    lane_of = lax.broadcasted_iota(jnp.int32, (1, capacity), 1)
    lists = []
    for rr in range(row_total):
        live = lane_of < jnp.broadcast_to(send_count[0, :, rr : rr + 1], (1, capacity))
        lists.append(jnp.where(live, send_list[0, 0, rr : rr + 1, :], -1))
    slots_held = slot_position[0]
    blocks = block_slot[...]
    for rr in range(row_total):
        meta[rr] = jnp.zeros((META_ROWS, LANES), jnp.int32)
        for j in (-1, 0, 1):
            pick = min(max(rr + j, 0), row_total - 1)
            meta[rr, j + 1 : j + 2, 0:capacity] = lists[pick]
        meta[rr, SSP_ROW : SSP_ROW + 1, 0 : slots_held.shape[1]] = slots_held
        meta[rr, BSI_ROW : BSI_ROW + block_rows, 0:block_cols] = blocks
    for e in range(events):
        for half in range(halves):
            at = e * halves + half
            meta_levels[at : at + 1, :] = sections[e : e + 1, half * LANES : (half + 1) * LANES]

    cols_seen = 1 + (k > 0).astype(jnp.int32) + (k < col_total - 1).astype(jnp.int32)
    pl.semaphore_wait(barrier, row_total * cols_seen - 1)

    def meta_copies(rr, dc, arriving):
        at = (rr, 1 + dc) if arriving else (r, 1 - dc)
        return [
            pltpu.make_async_remote_copy(
                src_ref=source,
                dst_ref=target.at[at],
                send_sem=meta_send.at[which, rr, dc + 1],
                recv_sem=meta_recv.at[(which,) + at],
                device_id={"row": rr, "col": k + dc},
                device_id_type=pl.DeviceIdType.MESH,
            )
            for which, (source, target) in enumerate(
                ((meta.at[rr], landed), (meta_levels, landed_levels))
            )
        ]

    def strip_copy(index, array, dr, dc):
        src_rows, dst_rows = row_spans(dr, tile_rows)
        src_cols, dst_cols = col_spans(dc, tile_cols)
        source = terrain[array]
        return pltpu.make_async_remote_copy(
            src_ref=source.at[src_rows, src_cols],
            dst_ref=ext.at[array, dst_rows, dst_cols],
            send_sem=strip_send.at[index, array],
            recv_sem=strip_recv.at[index, array],
            device_id={"row": r - dr, "col": k - dc},
            device_id_type=pl.DeviceIdType.MESH,
        )

    def tile_exists(dr, dc):
        there = jnp.logical_and(r + dr >= 0, r + dr < row_total)
        return jnp.logical_and(there, col_exists(dc))

    for rr in range(row_total):
        for dc in (-1, 0, 1):
            @pl.when(partner(rr, dc))
            def _():
                for copy in meta_copies(rr, dc, False):
                    copy.start()
    for index, (dr, dc) in enumerate(REGIONS):
        @pl.when(tile_exists(-dr, -dc))
        def _():
            for array in range(3):
                strip_copy(index, array, dr, dc).start()
    meta_own = [
        pltpu.make_async_copy(meta.at[r], landed.at[r, 1], meta_own_sem.at[0]),
        pltpu.make_async_copy(meta_levels, landed_levels.at[r, 1], meta_own_sem.at[1]),
    ]
    for copy in meta_own:
        copy.start()

    lane = lax.broadcasted_iota(jnp.int32, (SUBLANES, LANES), 1)
    near = lane < LANES // 2
    has_east = k < col_total - 1
    has_west = k > 0
    has_north = r > 0
    has_south = r < row_total - 1

    def section(dr, kc, row, col):
        rr = jnp.clip(r + dr, 0, row_total - 1)
        slot = table[rr, kc, BSI_ROW + row, col]
        place = table[rr, kc, SSP_ROW, slot]
        src = place // capacity
        local = table[src, kc, dr + 1, place % capacity]
        pick = jnp.maximum(local, 0)
        return [
            jnp.where(
                local >= 0,
                table_levels[src, kc, e * halves + pick // LANES, pick % LANES],
                jnp.float32(DRY_SECTION),
            )
            for e in range(events)
        ]

    lane_ok = jnp.where(near, has_east.astype(jnp.int32), has_west.astype(jnp.int32)) > 0

    row_id = lax.broadcasted_iota(jnp.int32, (SUBLANES, LANES), 0)
    upper = row_id < SUBLANES // 2

    south_near = own_tiles

    def tile_place(t):
        if t < own_tiles:
            return 0, t
        if t < own_tiles + halo_tiles:
            return 1, t - own_tiles
        return -1, t - halo_tiles - halo_tiles

    def inside(flag):
        return jnp.broadcast_to(flag.astype(jnp.int32), (SUBLANES, LANES))

    def keep_of(t, seam=False):
        dr = tile_place(t)[0]
        if seam:
            full = jnp.where(upper, inside(has_south), inside(has_north)) > 0
        elif dr == 0:
            return None, lane_ok
        else:
            full = inside(has_south if dr == 1 else has_north) > 0
        return full, jnp.logical_and(full, lane_ok)

    def masked(x, t, seam=False):
        full, side = keep_of(t, seam)
        body = x[:, :tile_cols]
        tail = jnp.where(side, x[:, tile_cols:], 0.0)
        if full is not None:
            body = jnp.where(jnp.concatenate([full] * (tile_cols // LANES), 1), body, 0.0)
        return jnp.concatenate([body, tail], 1)

    def span(t):
        return pl.ds(t * SUBLANES, SUBLANES)

    def beside(array, t):
        return jnp.where(
            near,
            ext[array, span(t), tile_cols : tile_cols + LANES],
            ext[array, span(t), tile_cols + LANES : tile_cols + 2 * LANES],
        )

    def keep(mask, x):
        return x if mask is None else jnp.where(mask, x, 0.0)

    def repeated(mask):
        return None if mask is None else jnp.concatenate([mask] * (tile_cols // LANES), 1)

    def set_terrain(t, mask, values, lanes):
        height, low, rough = values
        bed[span(t), lanes] = keep(mask, SCALE * (height + low))
        drag[span(t), lanes] = keep(mask, DRAG_SCALE * (rough * rough))

    main = slice(0, tile_cols)
    side = slice(tile_cols, width)

    def set_main(t):
        mask = repeated(keep_of(t)[0])
        set_terrain(t, mask, [ext[array, span(t), main] for array in range(3)], main)

    def set_depth(t):
        dr, row = tile_place(t)
        mask = keep_of(t)[0]
        for col in range(block_cols):
            lanes = slice(col * LANES, (col + 1) * LANES)
            height = ext[0, span(t), lanes]
            for e, level in enumerate(section(dr, 1, row, col)):
                value = SCALE * jnp.maximum(level - height, 0.0)
                if dr == 0:
                    hand_depth[e, span(t), lanes] = value
                depth[e, span(t), lanes] = keep(mask, value)

    for t in range(tiles):
        for e in range(events):
            east[e, span(t), :] = jnp.zeros((SUBLANES, width), jnp.float32)
            south[e, span(t), :] = jnp.zeros((SUBLANES, width), jnp.float32)
    for copy in own_copies:
        copy.wait()
    for t in range(own_tiles):
        set_main(t)

    for copy in meta_own:
        copy.wait()
    for rr in range(row_total):
        for dc in (-1, 0, 1):
            @pl.when(partner(rr, dc))
            def _():
                for copy in meta_copies(rr, dc, True):
                    copy.wait_recv()
    tables = []
    for kc in range(3):
        held = 1 if kc == 1 else jnp.where(col_exists(kc - 1), kc, 1)
        for which, (source, target) in enumerate(
            ((landed, table), (landed_levels, table_levels))
        ):
            tables.append(
                pltpu.make_async_copy(
                    source.at[:, held], target.at[:, kc], table_sem.at[which, kc]
                )
            )
    for copy in tables:
        copy.start()
    for copy in tables:
        copy.wait()
    for t in range(own_tiles):
        set_depth(t)

    side_levels = []
    for t in range(tiles):
        dr, row = tile_place(t)
        side_levels.append((section(dr, 2, row, 0), section(dr, 0, row, block_cols - 1)))

    for index, (dr, dc) in enumerate(REGIONS):
        @pl.when(tile_exists(dr, dc))
        def _():
            for array in range(3):
                strip_copy(index, array, dr, dc).wait_recv()
    for t in range(own_tiles, tiles):
        set_main(t)
        set_depth(t)
    for t in range(tiles):
        mask = keep_of(t)[1]
        values = [beside(array, t) for array in range(3)]
        set_terrain(t, mask, values, side)
        for e in range(events):
            level = jnp.where(near, side_levels[t][0][e], side_levels[t][1][e])
            depth[e, span(t), side] = keep(
                mask, SCALE * jnp.maximum(level - values[0], 0.0)
            )

    wide_row = lax.broadcasted_iota(jnp.int32, (SUBLANES, width), 0)
    last_row = wide_row == SUBLANES - 1
    first_row = wide_row == 0

    def up(x):
        return pltpu.roll(x, SUBLANES - 1, 0)

    def down(x):
        return pltpu.roll(x, 1, 0)

    def left(x):
        return pltpu.roll(x, width - 1, 1)

    def right(x):
        return pltpu.roll(x, 1, 1)

    for t in range(tiles):
        here = bed[span(t), :]
        after = bed[span((t + 1) % tiles), :]
        top_east[span(t), :] = jnp.maximum(here, left(here))
        top_south[span(t), :] = jnp.maximum(here, jnp.where(last_row, up(after), up(here)))

    def face(flow, here, beyond, top, rough):
        thick = jnp.maximum(here, beyond) - top
        power = jnp.exp2((-7.0 / 3.0) * jnp.log2(jnp.maximum(thick, SCALE * DEPTH_FLOOR)))
        pushed = flow - thick * (beyond - here)
        return pushed * pl.reciprocal(1.0 + rough * jnp.abs(flow) * power, approx=True)

    def step_ring(ring, seam):
        last = ring[-1]
        for e in range(events):
            def level(t):
                water = depth[e, span(t), :]
                here = water + bed[span(t), :]
                return water, here, up(here)

            def go_south(t, here, here_up, next_up):
                return face(
                    south[e, span(t), :], here, jnp.where(last_row, next_up, here_up),
                    top_south[span(t), :], drag[span(t), :],
                )

            final = level(last)
            now = level(ring[0])
            final_south = go_south(last, final[1], final[2], now[2])
            south_above = down(final_south)
            for place, t in enumerate(ring):
                water, here, here_up = now
                if t == last:
                    new_south = final_south
                else:
                    after = ring[place + 1]
                    now = final if after == last else level(after)
                    new_south = go_south(t, here, here_up, now[2])
                new_east = face(
                    east[e, span(t), :], here, left(here), top_east[span(t), :], drag[span(t), :]
                )
                south_down = down(new_south)
                change = (right(new_east) - new_east) + (
                    jnp.where(first_row, south_above, south_down) - new_south
                )
                depth[e, span(t), :] = masked(jnp.maximum(water + change, 0.0), t, t == seam)
                east[e, span(t), :] = masked(new_east, t, t == seam)
                south[e, span(t), :] = masked(new_south, t, t == seam)
                south_above = south_down

    def merge(near_tile, far_tile):
        half = wide_row < SUBLANES // 2
        for ref in (bed, top_east, top_south, drag):
            ref[span(near_tile), :] = jnp.where(half, ref[span(near_tile), :], ref[span(far_tile), :])
        for ref in (depth, east, south):
            for e in range(events):
                ref[e, span(near_tile), :] = jnp.where(
                    half, ref[e, span(near_tile), :], ref[e, span(far_tile), :]
                )

    def run(ring, seam):
        def one(turn, carry):
            step_ring(ring, seam)
            return carry

        lax.fori_loop(0, SUBLANES // 2, one, 0)

    slots = list(range(tiles))
    for depth_tiles in range(halo_tiles, 0, -1):
        souths = slots[south_near : south_near + depth_tiles]
        norths = slots[tiles - depth_tiles :]
        own = slots[:own_tiles]
        run(own + souths + norths, None)
        merge(souths[-1], norths[0])
        run(own + souths + norths[1:], souths[-1])

    for e in range(events):
        final_depth[e] = depth[e, 0:tile_rows, 0:tile_cols]

    for index, (dr, dc) in enumerate(REGIONS):
        @pl.when(tile_exists(-dr, -dc))
        def _():
            for array in range(3):
                strip_copy(index, array, dr, dc).wait_send()
    for rr in range(row_total):
        for dc in (-1, 0, 1):
            @pl.when(partner(rr, dc))
            def _():
                for copy in meta_copies(rr, dc, False):
                    copy.wait_send()


def body(
    row_total, col_total,
    sections, send_list, send_count, slot_sender_position, block_slot_index, hand, drain, manning,
):
    events, catch_local = sections.shape
    tile_rows, tile_cols = hand.shape
    vmem = pl.BlockSpec(memory_space=pltpu.VMEM)
    hbm = pl.BlockSpec(memory_space=pltpu.HBM)
    padded_rows = tile_rows + 2 * HALO
    width = tile_cols + LANES
    level_rows = events * (catch_local // LANES)
    state = pltpu.VMEM((events, padded_rows, width), jnp.float32)
    fixed = pltpu.VMEM((padded_rows, width), jnp.float32)
    out = jax.ShapeDtypeStruct((events, tile_rows, tile_cols), jnp.float32)
    landing = (row_total, 3, META_ROWS, LANES)
    landing_levels = (row_total, 3, level_rows, LANES)
    start, end = pl.pallas_call(
        functools.partial(flood_kernel, row_total, col_total),
        out_shape=(out, out),
        in_specs=[hbm] * 8,
        out_specs=(vmem, vmem),
        scratch_shapes=[
            pltpu.VMEM(x.shape, x.dtype)
            for x in (sections, send_list, send_count, slot_sender_position, block_slot_index)
        ]
        + [pltpu.SemaphoreType.DMA((5,))]
        + [
            pltpu.VMEM((3, padded_rows, tile_cols + 2 * LANES), jnp.float32),
            pltpu.VMEM((row_total, META_ROWS, LANES), jnp.int32),
            pltpu.VMEM((level_rows, LANES), jnp.float32),
            pltpu.VMEM(landing, jnp.int32),
            pltpu.VMEM(landing_levels, jnp.float32),
            pltpu.SMEM(landing, jnp.int32),
            pltpu.SMEM(landing_levels, jnp.float32),
        ]
        + [state] * 3
        + [fixed] * 4
        + [
            pltpu.SemaphoreType.DMA((len(REGIONS), 3)),
            pltpu.SemaphoreType.DMA((len(REGIONS), 3)),
            pltpu.SemaphoreType.DMA((2, row_total, 3)),
            pltpu.SemaphoreType.DMA((2, row_total, 3)),
            pltpu.SemaphoreType.DMA((3,)),
            pltpu.SemaphoreType.DMA((2,)),
            pltpu.SemaphoreType.DMA((2, 3)),
        ],
        compiler_params=pltpu.CompilerParams(
            collective_id=0, has_side_effects=True, vmem_limit_bytes=VMEM_BYTES
        ),
        name="flood",
    )(*[
        pltpu.with_memory_space_constraint(x, pltpu.HBM)
        for x in (
            sections, send_list, send_count, slot_sender_position, block_slot_index, hand, drain, manning,
        )
    ])
    return start * (1.0 / SCALE), end * (1.0 / SCALE)


def solution(mesh):
    return jax.shard_map(
        functools.partial(body, mesh.shape["row"], mesh.shape["col"]),
        mesh=mesh,
        in_specs=(
            P("evt", ("grp", "row", "col")),
            P(("grp", "row"), "col", None, None),
            P(("grp", "row"), "col", None),
            P(("grp", "row"), "col", None),
            P(("grp", "row"), "col"),
            P(("grp", "row"), "col"),
            P(("grp", "row"), "col"),
            P(("grp", "row"), "col"),
        ),
        out_specs=(P("evt", ("grp", "row"), "col"), P("evt", ("grp", "row"), "col")),
        check_vma=False,
    )
```

profile of v0, /device:TPU:0, one launch (start us, length us, event | category | flops | bytes accessed | tf_op | source)
XLA Modules:
  0.0 30.2 jit_solution(8570919430507568298)
XLA Ops:
  0.6 28.8 %flood.1 = (f32[2,32,1024]{2,1,0:T(8,128)S(1)}, f32[2,32,1024]{2,1,0:T(8,128)S(1)}) custom-call(f32[2,256]{1,0:T(2,128)} %sections_in.1, s32[1,1,4,64]{3,2,1,0:T(4,128)} %send_list_in.1, s32[1,1,4]{2,1,0:T(1,128)} %send_count_in.1, s32[1,1,32]{2,1,0:T(1,128)} %slot_position_in.1, s32[4,8]{1,0:T(4,128)} %block_slot_in.1, f32[32,1024]{1,0:T(8,128)} %hand.1, ...), custom_call_target="tpu_custom_call" | custom-call | tf_op jit(solution)/shard_map/flood/pallas_call | solution.py:461
  29.4 0.8 %broadcast_multiply_fusion = (f32[2,32,1024]{2,1,0:T(8,128)}, f32[2,32,1024]{2,1,0:T(8,128)}) fusion(f32[2,32,1024]{2,1,0:T(8,128)S(1)} %get-tuple-element.5, f32[2,32,1024]{2,1,0:T(8,128)S(1)} %get-tuple-element.4), kind=kLoop, calls=%fused_computation | loop fusion | flops 131072 | bytes 1048576 | tf_op jit(solution)/shard_map/mul | solution.py:501
where the time goes:
time: 30.4 us; the launch traced here: 30.2 us
  Pallas kernels  28.8 us (95%)
  other arithmetic  0.84 us (3%)
  between operations  0.64 us (2%)
    pallas_call x1, Pallas kernels, body(): pl.pallas_call(functools.partial(flood_kernel, row_total, col_total), out...  28.8 us
    mul x1, other arithmetic, body(): return (start * (1.0 / SCALE), end * (1.0 / SCALE))  0.84 us

commit v1 on v0

v1 whole, which is shorter than its diff:
```python
import functools

import jax
import jax.numpy as jnp
from jax import lax
from jax.experimental import pallas as pl
from jax.experimental.pallas import tpu as pltpu
from jax.sharding import PartitionSpec as P

STEPS = 16
GRAVITY = 9.81
TIMESTEP = 0.4
SPACING = 10.0
DEPTH_FLOOR = 0.05
DRY_SECTION = -1000.0

VMEM_BYTES = 24 * 1024 * 1024
LANES = 128
SUBLANES = 8
HALO = STEPS
SCALE = GRAVITY * TIMESTEP * TIMESTEP / (SPACING * SPACING)
DRAG_SCALE = (
    GRAVITY * TIMESTEP * SCALE ** (7.0 / 3.0) / (SCALE * TIMESTEP / SPACING)
)
REGIONS = tuple(
    (dr, dc) for dr in (-1, 0, 1) for dc in (-1, 0, 1) if (dr, dc) != (0, 0)
)
EDGE_STEPS = ((6, 7), (5, 9))
INNER_STEPS = ((8, 3), (7, 4), (6, 4), (5, 5))


def phases(has_north, has_south, own_tiles):
    if has_north and has_south:
        return [
            (-(tiles - own_tiles) * SUBLANES // 2, tiles, steps) for tiles, steps in INNER_STEPS
        ]
    return [
        (-(tiles - own_tiles) * SUBLANES if has_north else 0, tiles, steps)
        for tiles, steps in EDGE_STEPS
    ]


def row_spans(dr, tile_rows):
    if dr == -1:
        return pl.ds(tile_rows - HALO, HALO), pl.ds(0, HALO)
    if dr == 1:
        return pl.ds(0, HALO), pl.ds(HALO + tile_rows, HALO)
    return pl.ds(0, tile_rows), pl.ds(HALO, tile_rows)


def col_spans(dc, tile_cols):
    if dc == -1:
        return pl.ds(tile_cols - LANES, LANES), pl.ds(tile_cols + LANES, LANES)
    if dc == 1:
        return pl.ds(0, LANES), pl.ds(tile_cols, LANES)
    return pl.ds(0, tile_cols), pl.ds(0, tile_cols)


def pick_lanes(x, index):
    return jnp.take_along_axis(x, index, axis=1, mode="promise_in_bounds")


def flood_kernel(
    row_total, col_total,
    sections_in, send_list_in, send_count_in, slot_position_in, block_slot_in, hand, drain, manning,
    hand_depth, final_depth,
    sections, send_list, send_count, slot_position, block_slot,
    ext, lists, flat, slots, message, landed, place, where_held,
    bed_rows, drag_rows, rows, surface, east, south, fixed,
    small_sem, own_sem, strip_send, strip_recv, level_send, level_recv, place_send, place_recv, later_sem,
):
    r = lax.axis_index("row")
    k = lax.axis_index("col")
    tile_rows, tile_cols = hand.shape
    events, catch_local = sections.shape
    capacity = send_list.shape[3]
    block_rows, block_cols = block_slot.shape
    blocks = block_rows * block_cols
    cols = tile_cols // LANES
    width = tile_cols + LANES
    own_tiles = tile_rows // SUBLANES
    halo_tiles = HALO // SUBLANES
    terrain = (hand, drain, manning)

    def row_exists(dr):
        return jnp.logical_and(r + dr >= 0, r + dr < row_total)

    def col_exists(dc):
        return jnp.logical_and(k + dc >= 0, k + dc < col_total)

    def tile_exists(dr, dc):
        if dr == 0:
            return col_exists(dc)
        if dc == 0:
            return row_exists(dr)
        return jnp.logical_and(row_exists(dr), col_exists(dc))

    def as_int(flag):
        return flag.astype(jnp.int32)

    earlier = ((-1, -1), (-1, 0), (-1, 1), (0, -1))
    later = ((1, -1), (1, 0), (1, 1), (0, 1))
    barrier = pltpu.get_barrier_semaphore()

    def tell(semaphore, dr, dc):
        pl.semaphore_signal(
            semaphore, inc=1, device_id={"row": r + dr, "col": k + dc},
            device_id_type=pl.DeviceIdType.MESH,
        )

    for dr, dc in later:
        @pl.when(tile_exists(dr, dc))
        def _():
            tell(barrier, dr, dc)

    small_copies = [
        pltpu.make_async_copy(source, target, small_sem.at[at])
        for at, (source, target) in enumerate((
            (sections_in, sections), (send_list_in, send_list), (send_count_in, send_count),
            (slot_position_in, slot_position), (block_slot_in, block_slot),
        ))
    ]
    own_copies = [
        pltpu.make_async_copy(
            terrain[array], ext.at[array, pl.ds(HALO, tile_rows), pl.ds(0, tile_cols)],
            own_sem.at[array],
        )
        for array in range(3)
    ]
    for copy in small_copies + own_copies:
        copy.start()

    lane = lax.broadcasted_iota(jnp.int32, (SUBLANES, LANES), 1)
    row_id = lax.broadcasted_iota(jnp.int32, (SUBLANES, LANES), 0)
    near = lane < LANES // 2
    lists[...] = jnp.zeros(lists.shape, jnp.int32)
    flat[...] = jnp.zeros(flat.shape, jnp.int32)
    slots[...] = jnp.zeros(slots.shape, jnp.int32)
    for copy in small_copies:
        copy.wait()

    lane_of = lax.broadcasted_iota(jnp.int32, (1, capacity), 1)
    for rr in range(row_total):
        live = lane_of < jnp.broadcast_to(send_count[0, :, rr : rr + 1], (1, capacity))
        held = jnp.where(live, send_list[0, 0, rr : rr + 1, :], -1)
        for e in range(events):
            lists[rr : rr + 1, e * capacity : (e + 1) * capacity] = held
    list_rows = lists.shape[0]
    lane_tall = lax.broadcasted_iota(jnp.int32, (list_rows, LANES), 1)
    wanted = lists[...]
    local = jnp.maximum(wanted, 0)
    values = jnp.full((list_rows, LANES), DRY_SECTION, jnp.float32)
    for half in range(catch_local // LANES):
        mine = jnp.logical_and(wanted >= half * LANES, wanted < (half + 1) * LANES)
        for e in range(events):
            source = jnp.broadcast_to(
                sections[e : e + 1, half * LANES : (half + 1) * LANES], (list_rows, LANES)
            )
            found = pick_lanes(source, jnp.bitwise_and(local, LANES - 1))
            of_event = jnp.logical_and(lane_tall >= e * capacity, lane_tall < (e + 1) * capacity)
            values = jnp.where(jnp.logical_and(mine, of_event), found, values)
    for rr in range(row_total):
        message[rr] = jnp.full((SUBLANES, LANES), DRY_SECTION, jnp.float32)
        for j in (-1, 0, 1):
            pick = min(max(rr + j, 0), row_total - 1)
            message[rr, j + 1 : j + 2, :] = values[pick : pick + 1, :]

    ahead = sum(as_int(tile_exists(dr, dc)) for dr, dc in earlier) + as_int(r >= 2)

    @pl.when(ahead > 0)
    def _():
        pl.semaphore_wait(barrier, ahead)

    @pl.when(jnp.logical_and(r >= 1, r + 1 < row_total))
    def _():
        tell(barrier, 1, 0)

    for dr, dc in earlier:
        @pl.when(tile_exists(dr, dc))
        def _():
            tell(later_sem, dr, dc)

    def level_copy(rr, dc, arriving):
        at = (rr, 1 + dc) if arriving else (r, 1 - dc)
        return pltpu.make_async_remote_copy(
            src_ref=message.at[rr],
            dst_ref=landed.at[at],
            send_sem=level_send.at[rr, dc + 1],
            recv_sem=level_recv.at[at],
            device_id={"row": rr, "col": k + dc},
            device_id_type=pl.DeviceIdType.MESH,
        )

    def place_copy(index, dr, dc):
        return pltpu.make_async_remote_copy(
            src_ref=place,
            dst_ref=where_held.at[1 + dr, 1 + dc],
            send_sem=place_send.at[index],
            recv_sem=place_recv.at[index],
            device_id={"row": r - dr, "col": k - dc},
            device_id_type=pl.DeviceIdType.MESH,
        )

    def strip_copy(index, array, dr, dc):
        src_rows, dst_rows = row_spans(dr, tile_rows)
        src_cols, dst_cols = col_spans(dc, tile_cols)
        return pltpu.make_async_remote_copy(
            src_ref=terrain[array].at[src_rows, src_cols],
            dst_ref=ext.at[array, dst_rows, dst_cols],
            send_sem=strip_send.at[index, array],
            recv_sem=strip_recv.at[index, array],
            device_id={"row": r - dr, "col": k - dc},
            device_id_type=pl.DeviceIdType.MESH,
        )

    def send_levels(to_earlier):
        for rr in range(row_total):
            for dc in (-1, 0, 1):
                if to_earlier:
                    there = (rr <= r) if dc == -1 else (rr < r)
                else:
                    there = (rr >= r) if dc == 1 else (rr > r)
                if dc != 0:
                    there = jnp.logical_and(there, col_exists(dc))

                @pl.when(there)
                def _():
                    level_copy(rr, dc, False).start()

    def send_near(targets):
        for index, (dr, dc) in enumerate(REGIONS):
            if (-dr, -dc) in targets:
                @pl.when(tile_exists(-dr, -dc))
                def _():
                    place_copy(index, dr, dc).start()
                    for array in range(3):
                        strip_copy(index, array, dr, dc).start()

    send_levels(True)

    slots[0:1, 0 : slot_position.shape[2]] = slot_position[0]
    for e in range(events):
        for row in range(block_rows):
            at = e * blocks + row * block_cols
            flat[0:1, at : at + block_cols] = block_slot[row : row + 1, :]
    tile_shape = (SUBLANES, LANES)
    own_place = pick_lanes(
        jnp.broadcast_to(slots[0:1, :], tile_shape), jnp.broadcast_to(flat[0:1, :], tile_shape)
    )
    place[...] = own_place
    where_held[1, 1] = own_place

    send_near(earlier)
    behind = sum(as_int(tile_exists(dr, dc)) for dr, dc in later) + as_int(r + 2 < row_total)

    @pl.when(behind > 0)
    def _():
        pl.semaphore_wait(later_sem, behind)

    @pl.when(jnp.logical_and(r >= 1, r + 1 < row_total))
    def _():
        tell(later_sem, -1, 0)

    send_levels(False)
    send_near(later)
    landed[r, 1] = message[r]

    lane_ok = jnp.where(near, as_int(col_exists(1)), as_int(col_exists(-1))) > 0
    wide_row = lax.broadcasted_iota(jnp.int32, (SUBLANES, width), 0)
    last_row = wide_row == SUBLANES - 1
    first_row = wide_row == 0

    def span(t):
        return pl.ds(t * SUBLANES, SUBLANES)

    def piece(j):
        return slice(j * LANES, (j + 1) * LANES)

    def up(x):
        return pltpu.roll(x, SUBLANES - 1, 0)

    def down(x):
        return pltpu.roll(x, 1, 0)

    def left(x):
        return pltpu.roll(x, width - 1, 1)

    def right(x):
        return pltpu.roll(x, 1, 1)

    def guard(x):
        return jnp.concatenate(
            [x[:, :tile_cols], jnp.where(lane_ok, x[:, tile_cols:], 0.0)], 1
        )

    def beside(array, t):
        return jnp.where(
            near,
            ext[array, span(t), tile_cols : tile_cols + LANES],
            ext[array, span(t), tile_cols + LANES : tile_cols + 2 * LANES],
        )

    def set_terrain(t, side):
        if side:
            height, low, rough = [beside(array, t) for array in range(3)]
            bed_rows[cols, span(t), :] = jnp.where(lane_ok, SCALE * (height + low), 0.0)
            drag_rows[cols, span(t), :] = jnp.where(lane_ok, DRAG_SCALE * (rough * rough), 0.0)
            return
        for j in range(cols):
            height, low, rough = [ext[array, span(t), piece(j)] for array in range(3)]
            bed_rows[j, span(t), :] = SCALE * (height + low)
            drag_rows[j, span(t), :] = DRAG_SCALE * (rough * rough)

    def spread(ref, first, tiles, t):
        return jnp.concatenate(
            [ref[j, pl.ds(first + t, SUBLANES, stride=tiles), :] for j in range(cols + 1)], 1
        )

    def gather_back(ref, first, tiles, t, x):
        for j in range(cols + 1):
            ref[j, pl.ds(first + t, SUBLANES, stride=tiles), :] = x[:, piece(j)]

    def level_of(held, dr, lane_at):
        return jnp.broadcast_to(held[dr + 1 : dr + 2, lane_at : lane_at + 1], tile_shape)

    def face(flow, here, beyond, top, rough):
        thick = jnp.maximum(here, beyond) - top
        power = jnp.exp2((-7.0 / 3.0) * jnp.log2(jnp.maximum(thick, SCALE * DEPTH_FLOOR)))
        pushed = flow - thick * (beyond - here)
        return pushed * pl.reciprocal(1.0 + rough * jnp.abs(flow) * power, approx=True)

    def flood(has_north, has_south):
        plan = [(first + HALO, tiles, steps) for first, tiles, steps in phases(has_north, has_south, own_tiles)]
        row_tiles = range(
            0 if has_north else halo_tiles,
            halo_tiles + own_tiles + (halo_tiles if has_south else 0),
        )

        def below(bottom, x):
            x = up(x)
            return x if has_south else jnp.where(last_row, 0.0, x)

        for t in range(halo_tiles, halo_tiles + own_tiles):
            set_terrain(t, False)
        for index, (dr, dc) in enumerate(REGIONS):
            if (dr == -1 and not has_north) or (dr == 1 and not has_south):
                continue

            @pl.when(col_exists(dc))
            def _():
                for array in range(3):
                    strip_copy(index, array, dr, dc).wait_recv()
        for t in row_tiles:
            if t < halo_tiles or t >= halo_tiles + own_tiles:
                set_terrain(t, False)
            set_terrain(t, True)

        base = 0
        for first, tiles, _ in plan:
            start = spread(bed_rows, first, tiles, 0)
            here = start
            for t in range(tiles):
                after = below(True, start) if t == tiles - 1 else spread(bed_rows, first, tiles, t + 1)
                fixed[base + t, 0] = here
                fixed[base + t, 1] = jnp.maximum(here, left(here))
                fixed[base + t, 2] = jnp.maximum(here, after)
                fixed[base + t, 3] = spread(drag_rows, first, tiles, t)
                here = after
            base += tiles
        for t in range(plan[0][1]):
            for e in range(events):
                east[e, t] = jnp.zeros((SUBLANES, width), jnp.float32)
                south[e, t] = jnp.zeros((SUBLANES, width), jnp.float32)

        for index, (dr, dc) in enumerate(REGIONS):
            if (dr == -1 and not has_north) or (dr == 1 and not has_south):
                continue

            @pl.when(col_exists(dc))
            def _():
                place_copy(index, dr, dc).wait_recv()
        for rr in range(row_total):
            for dc in (-1, 0, 1):
                there = (rr != r) if dc == 0 else col_exists(dc)

                @pl.when(there)
                def _():
                    level_copy(rr, dc, True).wait_recv()

        event_shift = jnp.where(lane >= blocks, capacity, 0)
        levels = []
        for kc in range(3):
            placed = jnp.where(
                row_id == 0, where_held[0, kc], jnp.where(row_id == 1, where_held[1, kc], where_held[2, kc])
            )
            source = lax.shift_right_logical(placed, capacity.bit_length() - 1)
            at = jnp.bitwise_and(placed, capacity - 1) + event_shift
            level = jnp.full(tile_shape, DRY_SECTION, jnp.float32)
            for rr in range(row_total):
                level = jnp.where(source == rr, pick_lanes(landed[rr, kc], at), level)
            levels.append(level)

        for t in row_tiles:
            dr, row = 0, t - halo_tiles
            if t < halo_tiles:
                dr, row = -1, block_rows - halo_tiles + t
            elif row >= own_tiles:
                dr, row = 1, row - own_tiles
            side_height = beside(0, t)
            for e in range(events):
                at = e * blocks + row * block_cols
                for j in range(cols):
                    value = SCALE * jnp.maximum(
                        level_of(levels[1], dr, at + j) - ext[0, span(t), piece(j)], 0.0
                    )
                    if dr == 0:
                        hand_depth[e, span(row), piece(j)] = value
                    rows[0, e, j, span(t), :] = value + bed_rows[j, span(t), :]
                level = jnp.where(
                    near, level_of(levels[2], dr, at), level_of(levels[0], dr, at + block_cols - 1)
                )
                value = SCALE * jnp.maximum(level - side_height, 0.0) + bed_rows[cols, span(t), :]
                rows[0, e, cols, span(t), :] = jnp.where(lane_ok, value, 0.0)

        def one_step(base, tiles):
            end = tiles - 1
            for e in range(events):
                def go_south(t, here, beyond):
                    return face(south[e, t], here, beyond, fixed[base + t, 2], fixed[base + t, 3])

                start = surface[e, 0]
                final_south = go_south(end, surface[e, end], below(True, start))
                above = down(final_south)
                if not has_north:
                    above = jnp.where(first_row, (fixed[base, 0] - start) * start, above)
                here = start
                for t in range(tiles):
                    if t == end:
                        new_south = final_south
                        after = None
                    else:
                        after = surface[e, t + 1]
                        new_south = go_south(t, here, after)
                    new_east = face(
                        east[e, t], here, left(here), fixed[base + t, 1], fixed[base + t, 3]
                    )
                    change = (right(new_east) - new_east) + (above - new_south)
                    surface[e, t] = guard(jnp.maximum(here + change, fixed[base + t, 0]))
                    east[e, t] = guard(new_east)
                    south[e, t] = new_south
                    above = new_south
                    here = after

        base = 0
        for number, (first, tiles, steps) in enumerate(plan):
            if number > 0:
                old_first, old_tiles, _ = plan[number - 1]
                for e in range(events):
                    for which, ref in enumerate((surface, east, south)):
                        for t in range(old_tiles):
                            gather_back(rows.at[which, e], old_first, old_tiles, t, ref[e, t])
            for e in range(events):
                for which, ref in enumerate((surface, east, south)):
                    if number > 0 or which == 0:
                        for t in range(tiles):
                            ref[e, t] = spread(rows.at[which, e], first, tiles, t)

            def one(turn, carry, base=base, tiles=tiles):
                one_step(base, tiles)
                return carry

            lax.fori_loop(0, steps, one, 0)
            base += tiles
        first, tiles, _ = plan[-1]
        for e in range(events):
            for t in range(tiles):
                gather_back(rows.at[0, e], first, tiles, t, surface[e, t])
            for t in range(own_tiles):
                for j in range(cols):
                    at = span(halo_tiles + t)
                    final_depth[e, span(t), piece(j)] = rows[0, e, j, at, :] - bed_rows[j, at, :]

    for copy in own_copies:
        copy.wait()

    @pl.when(r == 0)
    def _():
        flood(False, True)

    @pl.when(jnp.logical_and(r > 0, r < row_total - 1))
    def _():
        flood(True, True)

    @pl.when(r == row_total - 1)
    def _():
        flood(True, False)

    for index, (dr, dc) in enumerate(REGIONS):
        @pl.when(tile_exists(-dr, -dc))
        def _():
            place_copy(index, dr, dc).wait_send()
            for array in range(3):
                strip_copy(index, array, dr, dc).wait_send()
    for rr in range(row_total):
        for dc in (-1, 0, 1):
            there = (rr != r) if dc == 0 else col_exists(dc)

            @pl.when(there)
            def _():
                level_copy(rr, dc, False).wait_send()


def body(
    row_total, col_total,
    sections, send_list, send_count, slot_sender_position, block_slot_index, hand, drain, manning,
):
    events = sections.shape[0]
    tile_rows, tile_cols = hand.shape
    vmem = pl.BlockSpec(memory_space=pltpu.VMEM)
    hbm = pl.BlockSpec(memory_space=pltpu.HBM)
    padded_rows = tile_rows + 2 * HALO
    padded_tiles = padded_rows // SUBLANES
    width = tile_cols + LANES
    pieces = width // LANES
    small = (sections, send_list, send_count, slot_sender_position, block_slot_index)
    list_rows = -(-row_total // SUBLANES) * SUBLANES
    fixed_tiles = max(
        sum(tiles for tiles, _ in EDGE_STEPS), sum(tiles for tiles, _ in INNER_STEPS)
    )
    by_rows = pltpu.VMEM((pieces, padded_rows, LANES), jnp.float32)
    state = pltpu.VMEM((events, padded_tiles, SUBLANES, width), jnp.float32)
    out = jax.ShapeDtypeStruct((events, tile_rows, tile_cols), jnp.float32)
    start, end = pl.pallas_call(
        functools.partial(flood_kernel, row_total, col_total),
        out_shape=(out, out),
        in_specs=[hbm] * 8,
        out_specs=(vmem, vmem),
        scratch_shapes=[pltpu.VMEM(x.shape, x.dtype) for x in small]
        + [
            pltpu.VMEM((3, padded_rows, tile_cols + 2 * LANES), jnp.float32),
            pltpu.VMEM((list_rows, LANES), jnp.int32),
            pltpu.VMEM((SUBLANES, LANES), jnp.int32),
            pltpu.VMEM((SUBLANES, LANES), jnp.int32),
            pltpu.VMEM((row_total, SUBLANES, LANES), jnp.float32),
            pltpu.VMEM((row_total, 3, SUBLANES, LANES), jnp.float32),
            pltpu.VMEM((SUBLANES, LANES), jnp.int32),
            pltpu.VMEM((3, 3, SUBLANES, LANES), jnp.int32),
            by_rows,
            by_rows,
            pltpu.VMEM((3, events, pieces, padded_rows, LANES), jnp.float32),
            state,
            state,
            state,
            pltpu.VMEM((fixed_tiles, 4, SUBLANES, width), jnp.float32),
            pltpu.SemaphoreType.DMA((len(small),)),
            pltpu.SemaphoreType.DMA((3,)),
            pltpu.SemaphoreType.DMA((len(REGIONS), 3)),
            pltpu.SemaphoreType.DMA((len(REGIONS), 3)),
            pltpu.SemaphoreType.DMA((row_total, 3)),
            pltpu.SemaphoreType.DMA((row_total, 3)),
            pltpu.SemaphoreType.DMA((len(REGIONS),)),
            pltpu.SemaphoreType.DMA((len(REGIONS),)),
            pltpu.SemaphoreType.REGULAR,
        ],
        compiler_params=pltpu.CompilerParams(
            collective_id=0, has_side_effects=True, vmem_limit_bytes=VMEM_BYTES
        ),
        name="flood",
    )(*[pltpu.with_memory_space_constraint(x, pltpu.HBM) for x in (*small, hand, drain, manning)])
    return start * (1.0 / SCALE), end * (1.0 / SCALE)


def solution(mesh):
    return jax.shard_map(
        functools.partial(body, mesh.shape["row"], mesh.shape["col"]),
        mesh=mesh,
        in_specs=(
            P("evt", ("grp", "row", "col")),
            P(("grp", "row"), "col", None, None),
            P(("grp", "row"), "col", None),
            P(("grp", "row"), "col", None),
            P(("grp", "row"), "col"),
            P(("grp", "row"), "col"),
            P(("grp", "row"), "col"),
            P(("grp", "row"), "col"),
        ),
        out_specs=(P("evt", ("grp", "row"), "col"), P("evt", ("grp", "row"), "col")),
        check_vma=False,
    )
```

time: 30.4 us -> 30.3 us (level)
  the two profiles are of different devices: /device:TPU:0 before, /device:TPU:8 now
where the time goes in v1:
time: 30.3 us; the launch traced here: 30.1 us
  Pallas kernels  28.7 us (95%)
  other arithmetic  0.84 us (3%)
  between operations  0.64 us (2%)
    pallas_call x1, Pallas kernels, body(): pl.pallas_call(functools.partial(flood_kernel, row_total, col_total), out...  28.7 us
    mul x1, other arithmetic, body(): return (start * (1.0 / SCALE), end * (1.0 / SCALE))  0.84 us

profile of v1, /device:TPU:8, one launch (start us, length us, event | category | flops | bytes accessed | tf_op | source)
XLA Modules:
  0.0 30.1 jit_solution(11143237652373277457)
XLA Ops:
  0.6 28.7 %flood.1 = (f32[2,32,1024]{2,1,0:T(8,128)S(1)}, f32[2,32,1024]{2,1,0:T(8,128)S(1)}) custom-call(f32[2,256]{1,0:T(2,128)} %sections_in.1, s32[1,1,4,64]{3,2,1,0:T(4,128)} %send_list_in.1, s32[1,1,4]{2,1,0:T(1,128)} %send_count_in.1, s32[1,1,32]{2,1,0:T(1,128)} %slot_position_in.1, s32[4,8]{1,0:T(4,128)} %block_slot_in.1, f32[32,1024]{1,0:T(8,128)} %hand.1, ...), custom_call_target="tpu_custom_call" | custom-call | tf_op jit(solution)/shard_map/flood/pallas_call | solution.py:533
  29.3 0.8 %broadcast_multiply_fusion = (f32[2,32,1024]{2,1,0:T(8,128)}, f32[2,32,1024]{2,1,0:T(8,128)}) fusion(f32[2,32,1024]{2,1,0:T(8,128)S(1)} %get-tuple-element.5, f32[2,32,1024]{2,1,0:T(8,128)S(1)} %get-tuple-element.4), kind=kLoop, calls=%fused_computation | loop fusion | flops 131072 | bytes 1048576 | tf_op jit(solution)/shard_map/mul | solution.py:570

commit v2 on v1

--- a/solution.py
+++ b/solution.py
@@ -26,7 +26,9 @@
     (dr, dc) for dr in (-1, 0, 1) for dc in (-1, 0, 1) if (dr, dc) != (0, 0)
 )
 EDGE_STEPS = ((6, 7), (5, 9))
-INNER_STEPS = ((8, 3), (7, 4), (6, 4), (5, 5))
+INNER_STEPS = ((8, 7), (6, 9))
+
+TOGETHER_TILES = 6
 
 
 def phases(has_north, has_south, own_tiles):
@@ -67,7 +69,7 @@
     sections, send_list, send_count, slot_position, block_slot,
     ext, lists, flat, slots, message, landed, place, where_held,
     bed_rows, drag_rows, rows, surface, east, south, fixed,
-    small_sem, own_sem, strip_send, strip_recv, level_send, level_recv, place_send, place_recv, later_sem,
+    small_sem, own_sem, strip_send, strip_recv, level_send, level_recv, place_send, place_recv, near_sem, far_sem,
 ):
     r = lax.axis_index("row")
     k = lax.axis_index("col")
@@ -102,16 +104,29 @@
     later = ((1, -1), (1, 0), (1, 1), (0, 1))
     barrier = pltpu.get_barrier_semaphore()
 
-    def tell(semaphore, dr, dc):
+    def is_earlier(rr, dc):
+        there = (rr <= r) if dc == -1 else (rr < r)
+        return there if dc == 0 else jnp.logical_and(there, col_exists(dc))
+
+    def is_later(rr, dc):
+        there = (rr >= r) if dc == 1 else (rr > r)
+        return there if dc == 0 else jnp.logical_and(there, col_exists(dc))
+
+    def is_near(rr, dc):
+        return jnp.logical_and(rr - r <= 1, r - rr <= 1)
+
+    partners = [(rr, dc) for rr in range(row_total) for dc in (-1, 0, 1)]
+
+    def tell(semaphore, rr, dc):
         pl.semaphore_signal(
-            semaphore, inc=1, device_id={"row": r + dr, "col": k + dc},
+            semaphore, inc=1, device_id={"row": rr, "col": k + dc},
             device_id_type=pl.DeviceIdType.MESH,
         )
 
-    for dr, dc in later:
-        @pl.when(tile_exists(dr, dc))
+    for rr, dc in partners:
+        @pl.when(is_later(rr, dc))
         def _():
-            tell(barrier, dr, dc)
+            tell(barrier, rr, dc)
 
     small_copies = [
         pltpu.make_async_copy(source, target, small_sem.at[at])
@@ -129,6 +144,21 @@
     ]
     for copy in small_copies + own_copies:
         copy.start()
+
+    ahead = sum(as_int(is_earlier(rr, dc)) for rr, dc in partners)
+
+    @pl.when(ahead > 0)
+    def _():
+        pl.semaphore_wait(barrier, ahead)
+
+    for rr, dc in partners:
+        @pl.when(jnp.logical_and(is_earlier(rr, dc), is_near(rr, dc)))
+        def _():
+            tell(near_sem, rr, dc)
+
+        @pl.when(jnp.logical_and(is_earlier(rr, dc), jnp.logical_not(is_near(rr, dc))))
+        def _():
+            tell(far_sem, rr, dc)
 
     lane = lax.broadcasted_iota(jnp.int32, (SUBLANES, LANES), 1)
     row_id = lax.broadcasted_iota(jnp.int32, (SUBLANES, LANES), 0)
@@ -165,21 +195,6 @@
             pick = min(max(rr + j, 0), row_total - 1)
             message[rr, j + 1 : j + 2, :] = values[pick : pick + 1, :]
 
-    ahead = sum(as_int(tile_exists(dr, dc)) for dr, dc in earlier) + as_int(r >= 2)
-
-    @pl.when(ahead > 0)
-    def _():
-        pl.semaphore_wait(barrier, ahead)
-
-    @pl.when(jnp.logical_and(r >= 1, r + 1 < row_total))
-    def _():
-        tell(barrier, 1, 0)
-
-    for dr, dc in earlier:
-        @pl.when(tile_exists(dr, dc))
-        def _():
-            tell(later_sem, dr, dc)
-
     def level_copy(rr, dc, arriving):
         at = (rr, 1 + dc) if arriving else (r, 1 - dc)
         return pltpu.make_async_remote_copy(
@@ -213,19 +228,11 @@
             device_id_type=pl.DeviceIdType.MESH,
         )
 
-    def send_levels(to_earlier):
-        for rr in range(row_total):
-            for dc in (-1, 0, 1):
-                if to_earlier:
-                    there = (rr <= r) if dc == -1 else (rr < r)
-                else:
-                    there = (rr >= r) if dc == 1 else (rr > r)
-                if dc != 0:
-                    there = jnp.logical_and(there, col_exists(dc))
-
-                @pl.when(there)
-                def _():
-                    level_copy(rr, dc, False).start()
+    def send_levels(chosen):
+        for rr, dc in partners:
+            @pl.when(chosen(rr, dc))
+            def _():
+                level_copy(rr, dc, False).start()
 
     def send_near(targets):
         for index, (dr, dc) in enumerate(REGIONS):
@@ -236,7 +243,7 @@
                     for array in range(3):
                         strip_copy(index, array, dr, dc).start()
 
-    send_levels(True)
+    send_levels(is_earlier)
 
     slots[0:1, 0 : slot_position.shape[2]] = slot_position[0]
     for e in range(events):
@@ -251,18 +258,20 @@
     where_held[1, 1] = own_place
 
     send_near(earlier)
-    behind = sum(as_int(tile_exists(dr, dc)) for dr, dc in later) + as_int(r + 2 < row_total)
+    behind = sum(as_int(tile_exists(dr, dc)) for dr, dc in later)
+    beyond = sum(as_int(is_later(rr, dc)) for rr, dc in partners) - behind
 
     @pl.when(behind > 0)
     def _():
-        pl.semaphore_wait(later_sem, behind)
-
-    @pl.when(jnp.logical_and(r >= 1, r + 1 < row_total))
+        pl.semaphore_wait(near_sem, behind)
+
+    send_near(later)
+
+    @pl.when(beyond > 0)
     def _():
-        tell(later_sem, -1, 0)
-
-    send_levels(False)
-    send_near(later)
+        pl.semaphore_wait(far_sem, beyond)
+
+    send_levels(is_later)
     landed[r, 1] = message[r]
 
     lane_ok = jnp.where(near, as_int(col_exists(1)), as_int(col_exists(-1))) > 0
@@ -422,9 +431,9 @@
                 value = SCALE * jnp.maximum(level - side_height, 0.0) + bed_rows[cols, span(t), :]
                 rows[0, e, cols, span(t), :] = jnp.where(lane_ok, value, 0.0)
 
-        def one_step(base, tiles):
+        def one_step(base, tiles, chosen):
             end = tiles - 1
-            for e in range(events):
+            for e in chosen:
                 def go_south(t, here, beyond):
                     return face(south[e, t], here, beyond, fixed[base + t, 2], fixed[base + t, 3])
 
@@ -466,10 +475,17 @@
                             ref[e, t] = spread(rows.at[which, e], first, tiles, t)
 
             def one(turn, carry, base=base, tiles=tiles):
-                one_step(base, tiles)
+                one_step(base, tiles, range(events))
                 return carry
 
-            lax.fori_loop(0, steps, one, 0)
+            def one_apart(turn, carry, base=base, tiles=tiles):
+                one_step(base, tiles, (lax.rem(turn, events),))
+                return carry
+
+            if tiles <= TOGETHER_TILES:
+                lax.fori_loop(0, steps, one, 0)
+            else:
+                lax.fori_loop(0, steps * events, one_apart, 0)
             base += tiles
         first, tiles, _ = plan[-1]
         for e in range(events):
@@ -561,6 +577,7 @@
             pltpu.SemaphoreType.DMA((len(REGIONS),)),
             pltpu.SemaphoreType.DMA((len(REGIONS),)),
             pltpu.SemaphoreType.REGULAR,
+            pltpu.SemaphoreType.REGULAR,
         ],
         compiler_params=pltpu.CompilerParams(
             collective_id=0, has_side_effects=True, vmem_limit_bytes=VMEM_BYTES

time: 30.3 us -> 27.1 us (0.89)
  the two profiles are of different devices: /device:TPU:8 before, /device:TPU:16 now
where the time goes in v2:
time: 27.1 us; the launch traced here: 26.9 us
  Pallas kernels  25.4 us (94%)
  other arithmetic  0.84 us (3%)
  between operations  0.64 us (2%)
    pallas_call x1, Pallas kernels, body(): pl.pallas_call(functools.partial(flood_kernel, row_total, col_total), out...  25.4 us
    mul x1, other arithmetic, body(): return (start * (1.0 / SCALE), end * (1.0 / SCALE))  0.84 us

profile of v2, /device:TPU:16, one launch (start us, length us, event | category | flops | bytes accessed | tf_op | source)
XLA Modules:
  0.0 26.9 jit_solution(3011916798479978451)
XLA Ops:
  0.6 25.4 %flood.1 = (f32[2,32,1024]{2,1,0:T(8,128)S(1)}, f32[2,32,1024]{2,1,0:T(8,128)S(1)}) custom-call(f32[2,256]{1,0:T(2,128)} %sections_in.1, s32[1,1,4,64]{3,2,1,0:T(4,128)} %send_list_in.1, s32[1,1,4]{2,1,0:T(1,128)} %send_count_in.1, s32[1,1,32]{2,1,0:T(1,128)} %slot_position_in.1, s32[4,8]{1,0:T(4,128)} %block_slot_in.1, f32[32,1024]{1,0:T(8,128)} %hand.1, ...), custom_call_target="tpu_custom_call" | custom-call | tf_op jit(solution)/shard_map/flood/pallas_call | solution.py:549
  26.1 0.8 %broadcast_multiply_fusion = (f32[2,32,1024]{2,1,0:T(8,128)}, f32[2,32,1024]{2,1,0:T(8,128)}) fusion(f32[2,32,1024]{2,1,0:T(8,128)S(1)} %get-tuple-element.5, f32[2,32,1024]{2,1,0:T(8,128)S(1)} %get-tuple-element.4), kind=kLoop, calls=%fused_computation | loop fusion | flops 131072 | bytes 1048576 | tf_op jit(solution)/shard_map/mul | solution.py:587

commit v3 on v2

--- a/solution.py
+++ b/solution.py
@@ -26,7 +26,7 @@
     (dr, dc) for dr in (-1, 0, 1) for dc in (-1, 0, 1) if (dr, dc) != (0, 0)
 )
 EDGE_STEPS = ((6, 7), (5, 9))
-INNER_STEPS = ((8, 7), (6, 9))
+INNER_STEPS = ((8, 3), (7, 4), (6, 4), (5, 5))
 
 TOGETHER_TILES = 6
 
@@ -63,16 +63,17 @@
 
 
 def flood_kernel(
-    row_total, col_total,
+    row_total, col_total, cores,
     sections_in, send_list_in, send_count_in, slot_position_in, block_slot_in, hand, drain, manning,
     hand_depth, final_depth,
     sections, send_list, send_count, slot_position, block_slot,
     ext, lists, flat, slots, message, landed, place, where_held,
     bed_rows, drag_rows, rows, surface, east, south, fixed,
-    small_sem, own_sem, strip_send, strip_recv, level_send, level_recv, place_send, place_recv, near_sem, far_sem,
+    small_sem, own_sem, strip_send, strip_recv, level_send, level_recv, place_send, place_recv, pass_send, pass_recv, near_sem, far_sem, sibling_sem,
 ):
     r = lax.axis_index("row")
     k = lax.axis_index("col")
+    core = lax.axis_index("evt")
     tile_rows, tile_cols = hand.shape
     events, catch_local = sections.shape
     capacity = send_list.shape[3]
@@ -83,6 +84,9 @@
     own_tiles = tile_rows // SUBLANES
     halo_tiles = HALO // SUBLANES
     terrain = (hand, drain, manning)
+    shared = cores == 2
+    share = tile_cols // 2 if shared else tile_cols
+    tall = tuple((index, dr) for index, (dr, dc) in enumerate(REGIONS) if dc == 0)
 
     def row_exists(dr):
         return jnp.logical_and(r + dr >= 0, r + dr < row_total)
@@ -127,6 +131,16 @@
         @pl.when(is_later(rr, dc))
         def _():
             tell(barrier, rr, dc)
+
+    def tell_sibling(semaphore):
+        pl.semaphore_signal(
+            semaphore, inc=1, device_id={"evt": 1 - core}, device_id_type=pl.DeviceIdType.MESH
+        )
+
+    if shared:
+        @pl.when(core == 0)
+        def _():
+            tell_sibling(barrier)
 
     small_copies = [
         pltpu.make_async_copy(source, target, small_sem.at[at])
@@ -146,10 +160,17 @@
         copy.start()
 
     ahead = sum(as_int(is_earlier(rr, dc)) for rr, dc in partners)
+    if shared:
+        ahead = ahead + as_int(core == 1)
 
     @pl.when(ahead > 0)
     def _():
         pl.semaphore_wait(barrier, ahead)
+
+    if shared:
+        @pl.when(core == 1)
+        def _():
+            tell_sibling(sibling_sem)
 
     for rr, dc in partners:
         @pl.when(jnp.logical_and(is_earlier(rr, dc), is_near(rr, dc)))
@@ -158,7 +179,46 @@
 
         @pl.when(jnp.logical_and(is_earlier(rr, dc), jnp.logical_not(is_near(rr, dc))))
         def _():
-            tell(far_sem, rr, dc)
+            tell(far_sem.at[r], rr, dc)
+
+    def strip_copy(index, array, dr, dc):
+        src_rows, dst_rows = row_spans(dr, tile_rows)
+        src_cols, dst_cols = col_spans(dc, tile_cols)
+        if dc == 0:
+            src_cols = dst_cols = pl.ds(pl.multiple_of(core * share, LANES) if shared else 0, share)
+        return pltpu.make_async_remote_copy(
+            src_ref=terrain[array].at[src_rows, src_cols],
+            dst_ref=ext.at[array, dst_rows, dst_cols],
+            send_sem=strip_send.at[index, array],
+            recv_sem=strip_recv.at[index, array],
+            device_id={"row": r - dr, "col": k - dc},
+            device_id_type=pl.DeviceIdType.MESH,
+        )
+
+    def pass_on(index, array, dr):
+        held = ext.at[
+            array, row_spans(dr, tile_rows)[1], pl.ds(pl.multiple_of(core * share, LANES), share)
+        ]
+        return pltpu.make_async_remote_copy(
+            src_ref=held,
+            dst_ref=held,
+            send_sem=pass_send.at[index, array],
+            recv_sem=pass_recv.at[index, array],
+            device_id={"evt": 1 - core},
+            device_id_type=pl.DeviceIdType.MESH,
+        )
+
+    def send_strips(targets):
+        for index, (dr, dc) in enumerate(REGIONS):
+            if (-dr, -dc) in targets:
+                @pl.when(tile_exists(-dr, -dc))
+                def _():
+                    for array in range(3):
+                        strip_copy(index, array, dr, dc).start()
+
+    @pl.when(r < row_total - 1)
+    def _():
+        send_strips(earlier)
 
     lane = lax.broadcasted_iota(jnp.int32, (SUBLANES, LANES), 1)
     row_id = lax.broadcasted_iota(jnp.int32, (SUBLANES, LANES), 0)
@@ -216,32 +276,18 @@
             device_id_type=pl.DeviceIdType.MESH,
         )
 
-    def strip_copy(index, array, dr, dc):
-        src_rows, dst_rows = row_spans(dr, tile_rows)
-        src_cols, dst_cols = col_spans(dc, tile_cols)
-        return pltpu.make_async_remote_copy(
-            src_ref=terrain[array].at[src_rows, src_cols],
-            dst_ref=ext.at[array, dst_rows, dst_cols],
-            send_sem=strip_send.at[index, array],
-            recv_sem=strip_recv.at[index, array],
-            device_id={"row": r - dr, "col": k - dc},
-            device_id_type=pl.DeviceIdType.MESH,
-        )
-
     def send_levels(chosen):
         for rr, dc in partners:
             @pl.when(chosen(rr, dc))
             def _():
                 level_copy(rr, dc, False).start()
 
-    def send_near(targets):
+    def send_place(targets):
         for index, (dr, dc) in enumerate(REGIONS):
             if (-dr, -dc) in targets:
                 @pl.when(tile_exists(-dr, -dc))
                 def _():
                     place_copy(index, dr, dc).start()
-                    for array in range(3):
-                        strip_copy(index, array, dr, dc).start()
 
     send_levels(is_earlier)
 
@@ -257,21 +303,33 @@
     place[...] = own_place
     where_held[1, 1] = own_place
 
-    send_near(earlier)
+    send_place(earlier)
+
+    @pl.when(r == row_total - 1)
+    def _():
+        send_strips(earlier)
+
     behind = sum(as_int(tile_exists(dr, dc)) for dr, dc in later)
-    beyond = sum(as_int(is_later(rr, dc)) for rr, dc in partners) - behind
 
     @pl.when(behind > 0)
     def _():
         pl.semaphore_wait(near_sem, behind)
 
-    send_near(later)
-
-    @pl.when(beyond > 0)
-    def _():
-        pl.semaphore_wait(far_sem, beyond)
-
-    send_levels(is_later)
+    send_levels(lambda rr, dc: jnp.logical_and(is_later(rr, dc), is_near(rr, dc)))
+    send_strips(later)
+    send_place(later)
+    reach = sum(as_int(col_exists(dc)) for dc in (-1, 0, 1))
+    for row in range(row_total):
+        @pl.when(row > r + 1)
+        def _():
+            pl.semaphore_wait(far_sem.at[row], reach)
+
+            for rr, dc in partners:
+                if rr == row:
+                    @pl.when(is_later(rr, dc))
+                    def _():
+                        level_copy(rr, dc, False).start()
+
     landed[r, 1] = message[r]
 
     lane_ok = jnp.where(near, as_int(col_exists(1)), as_int(col_exists(-1))) > 0
@@ -351,8 +409,19 @@
 
         for t in range(halo_tiles, halo_tiles + own_tiles):
             set_terrain(t, False)
+        halos = [(index, dr) for index, dr in tall if (has_north if dr == -1 else has_south)]
+        if shared:
+            @pl.when(core == 0)
+            def _():
+                pl.semaphore_wait(sibling_sem, 1)
+
+        for array in range(3):
+            for index, dr in halos:
+                strip_copy(index, array, dr, 0).wait_recv()
+                if shared:
+                    pass_on(index, array, dr).start()
         for index, (dr, dc) in enumerate(REGIONS):
-            if (dr == -1 and not has_north) or (dr == 1 and not has_south):
+            if dc == 0 or (dr == -1 and not has_north) or (dr == 1 and not has_south):
                 continue
 
             @pl.when(col_exists(dc))
@@ -360,9 +429,14 @@
                 for array in range(3):
                     strip_copy(index, array, dr, dc).wait_recv()
         for t in row_tiles:
+            set_terrain(t, True)
+        if shared:
+            for array in range(3):
+                for index, dr in halos:
+                    pass_on(index, array, dr).wait_recv()
+        for t in row_tiles:
             if t < halo_tiles or t >= halo_tiles + own_tiles:
                 set_terrain(t, False)
-            set_terrain(t, True)
 
         base = 0
         for first, tiles, _ in plan:
@@ -511,6 +585,12 @@
     def _():
         flood(True, False)
 
+    if shared:
+        for index, dr in tall:
+            @pl.when(row_exists(dr))
+            def _():
+                for array in range(3):
+                    pass_on(index, array, dr).wait_send()
     for index, (dr, dc) in enumerate(REGIONS):
         @pl.when(tile_exists(-dr, -dc))
         def _():
@@ -527,7 +607,7 @@
 
 
 def body(
-    row_total, col_total,
+    row_total, col_total, cores,
     sections, send_list, send_count, slot_sender_position, block_slot_index, hand, drain, manning,
 ):
     events = sections.shape[0]
@@ -547,7 +627,7 @@
     state = pltpu.VMEM((events, padded_tiles, SUBLANES, width), jnp.float32)
     out = jax.ShapeDtypeStruct((events, tile_rows, tile_cols), jnp.float32)
     start, end = pl.pallas_call(
-        functools.partial(flood_kernel, row_total, col_total),
+        functools.partial(flood_kernel, row_total, col_total, cores),
         out_shape=(out, out),
         in_specs=[hbm] * 8,
         out_specs=(vmem, vmem),
@@ -576,7 +656,10 @@
             pltpu.SemaphoreType.DMA((row_total, 3)),
             pltpu.SemaphoreType.DMA((len(REGIONS),)),
             pltpu.SemaphoreType.DMA((len(REGIONS),)),
+            pltpu.SemaphoreType.DMA((len(REGIONS), 3)),
+            pltpu.SemaphoreType.DMA((len(REGIONS), 3)),
             pltpu.SemaphoreType.REGULAR,
+            pltpu.SemaphoreType.REGULAR((row_total,)),
             pltpu.SemaphoreType.REGULAR,
         ],
         compiler_params=pltpu.CompilerParams(
@@ -589,7 +672,7 @@
 
 def solution(mesh):
     return jax.shard_map(
-        functools.partial(body, mesh.shape["row"], mesh.shape["col"]),
+        functools.partial(body, mesh.shape["row"], mesh.shape["col"], mesh.shape["evt"]),
         mesh=mesh,
         in_specs=(
             P("evt", ("grp", "row", "col")),

time: 27.1 us -> 25.2 us (0.930)
  the two profiles are of different devices: /device:TPU:16 before, /device:TPU:17 now
where the time goes in v3:
time: 25.2 us; the launch traced here: 25 us
  Pallas kernels  23.5 us (93%)
  other arithmetic  0.84 us (3%)
  between operations  0.64 us (3%)
    pallas_call x1, Pallas kernels, body(): pl.pallas_call(functools.partial(flood_kernel, row_total, col_total, core...  23.5 us
    mul x1, other arithmetic, body(): return (start * (1.0 / SCALE), end * (1.0 / SCALE))  0.84 us

profile of v3, /device:TPU:17, one launch (start us, length us, event | category | flops | bytes accessed | tf_op | source)
XLA Modules:
  0.0 25.0 jit_solution(1529753663595331297)
XLA Ops:
  0.6 23.5 %flood.1 = (f32[2,32,1024]{2,1,0:T(8,128)S(1)}, f32[2,32,1024]{2,1,0:T(8,128)S(1)}) custom-call(f32[2,256]{1,0:T(2,128)} %sections_in.1, s32[1,1,4,64]{3,2,1,0:T(4,128)} %send_list_in.1, s32[1,1,4]{2,1,0:T(1,128)} %send_count_in.1, s32[1,1,32]{2,1,0:T(1,128)} %slot_position_in.1, s32[4,8]{1,0:T(4,128)} %block_slot_in.1, f32[32,1024]{1,0:T(8,128)} %hand.1, ...), custom_call_target="tpu_custom_call" | custom-call | tf_op jit(solution)/shard_map/flood/pallas_call | solution.py:629
  24.1 0.8 %broadcast_multiply_fusion = (f32[2,32,1024]{2,1,0:T(8,128)}, f32[2,32,1024]{2,1,0:T(8,128)}) fusion(f32[2,32,1024]{2,1,0:T(8,128)S(1)} %get-tuple-element.5, f32[2,32,1024]{2,1,0:T(8,128)S(1)} %get-tuple-element.4), kind=kLoop, calls=%fused_computation | loop fusion | flops 131072 | bytes 1048576 | tf_op jit(solution)/shard_map/mul | solution.py:670

commit v4 on v3

--- a/solution.py
+++ b/solution.py
@@ -209,7 +209,7 @@
         )
 
     def send_strips(targets):
-        for index, (dr, dc) in enumerate(REGIONS):
+        for index, (dr, dc) in sorted(enumerate(REGIONS), key=lambda entry: entry[1][1] != 0):
             if (-dr, -dc) in targets:
                 @pl.when(tile_exists(-dr, -dc))
                 def _():
@@ -409,6 +409,11 @@
 
         for t in range(halo_tiles, halo_tiles + own_tiles):
             set_terrain(t, False)
+        for t in range(plan[0][1]):
+            for e in range(events):
+                east[e, t] = jnp.zeros((SUBLANES, width), jnp.float32)
+                south[e, t] = jnp.zeros((SUBLANES, width), jnp.float32)
+
         halos = [(index, dr) for index, dr in tall if (has_north if dr == -1 else has_south)]
         if shared:
             @pl.when(core == 0)
@@ -421,6 +426,66 @@
                 if shared:
                     pass_on(index, array, dr).start()
         for index, (dr, dc) in enumerate(REGIONS):
+            if (dr == -1 and not has_north) or (dr == 1 and not has_south):
+                continue
+
+            @pl.when(col_exists(dc))
+            def _():
+                place_copy(index, dr, dc).wait_recv()
+        for rr in range(row_total):
+            for dc in (-1, 0, 1):
+                there = (rr != r) if dc == 0 else col_exists(dc)
+
+                @pl.when(there)
+                def _():
+                    level_copy(rr, dc, True).wait_recv()
+
+        event_shift = jnp.where(lane >= blocks, capacity, 0)
+        levels = []
+        for kc in range(3):
+            placed = jnp.where(
+                row_id == 0, where_held[0, kc], jnp.where(row_id == 1, where_held[1, kc], where_held[2, kc])
+            )
+            source = lax.shift_right_logical(placed, capacity.bit_length() - 1)
+            at = jnp.bitwise_and(placed, capacity - 1) + event_shift
+            level = jnp.full(tile_shape, DRY_SECTION, jnp.float32)
+            for rr in range(row_total):
+                level = jnp.where(source == rr, pick_lanes(landed[rr, kc], at), level)
+            levels.append(level)
+
+        def block_at(e, t):
+            dr, row = 0, t - halo_tiles
+            if t < halo_tiles:
+                dr, row = -1, block_rows - halo_tiles + t
+            elif row >= own_tiles:
+                dr, row = 1, row - own_tiles
+            return dr, row, e * blocks + row * block_cols
+
+        def set_surface(t):
+            for e in range(events):
+                dr, row, at = block_at(e, t)
+                for j in range(cols):
+                    value = SCALE * jnp.maximum(
+                        level_of(levels[1], dr, at + j) - ext[0, span(t), piece(j)], 0.0
+                    )
+                    if dr == 0:
+                        hand_depth[e, span(row), piece(j)] = value
+                    rows[0, e, j, span(t), :] = value + bed_rows[j, span(t), :]
+
+        def set_side_surface(t):
+            side_height = beside(0, t)
+            for e in range(events):
+                dr, row, at = block_at(e, t)
+                level = jnp.where(
+                    near, level_of(levels[2], dr, at), level_of(levels[0], dr, at + block_cols - 1)
+                )
+                value = SCALE * jnp.maximum(level - side_height, 0.0) + bed_rows[cols, span(t), :]
+                rows[0, e, cols, span(t), :] = jnp.where(lane_ok, value, 0.0)
+
+        own_range = range(halo_tiles, halo_tiles + own_tiles)
+        for t in own_range:
+            set_surface(t)
+        for index, (dr, dc) in enumerate(REGIONS):
             if dc == 0 or (dr == -1 and not has_north) or (dr == 1 and not has_south):
                 continue
 
@@ -430,13 +495,15 @@
                     strip_copy(index, array, dr, dc).wait_recv()
         for t in row_tiles:
             set_terrain(t, True)
+            set_side_surface(t)
         if shared:
             for array in range(3):
                 for index, dr in halos:
                     pass_on(index, array, dr).wait_recv()
         for t in row_tiles:
-            if t < halo_tiles or t >= halo_tiles + own_tiles:
+            if t not in own_range:
                 set_terrain(t, False)
+                set_surface(t)
 
         base = 0
         for first, tiles, _ in plan:
@@ -450,61 +517,6 @@
                 fixed[base + t, 3] = spread(drag_rows, first, tiles, t)
                 here = after
             base += tiles
-        for t in range(plan[0][1]):
-            for e in range(events):
-                east[e, t] = jnp.zeros((SUBLANES, width), jnp.float32)
-                south[e, t] = jnp.zeros((SUBLANES, width), jnp.float32)
-
-        for index, (dr, dc) in enumerate(REGIONS):
-            if (dr == -1 and not has_north) or (dr == 1 and not has_south):
-                continue
-
-            @pl.when(col_exists(dc))
-            def _():
-                place_copy(index, dr, dc).wait_recv()
-        for rr in range(row_total):
-            for dc in (-1, 0, 1):
-                there = (rr != r) if dc == 0 else col_exists(dc)
-
-                @pl.when(there)
-                def _():
-                    level_copy(rr, dc, True).wait_recv()
-
-        event_shift = jnp.where(lane >= blocks, capacity, 0)
-        levels = []
-        for kc in range(3):
-            placed = jnp.where(
-                row_id == 0, where_held[0, kc], jnp.where(row_id == 1, where_held[1, kc], where_held[2, kc])
-            )
-            source = lax.shift_right_logical(placed, capacity.bit_length() - 1)
-            at = jnp.bitwise_and(placed, capacity - 1) + event_shift
-            level = jnp.full(tile_shape, DRY_SECTION, jnp.float32)
-            for rr in range(row_total):
-                level = jnp.where(source == rr, pick_lanes(landed[rr, kc], at), level)
-            levels.append(level)
-
-        for t in row_tiles:
-            dr, row = 0, t - halo_tiles
-            if t < halo_tiles:
-                dr, row = -1, block_rows - halo_tiles + t
-            elif row >= own_tiles:
-                dr, row = 1, row - own_tiles
-            side_height = beside(0, t)
-            for e in range(events):
-                at = e * blocks + row * block_cols
-                for j in range(cols):
-                    value = SCALE * jnp.maximum(
-                        level_of(levels[1], dr, at + j) - ext[0, span(t), piece(j)], 0.0
-                    )
-                    if dr == 0:
-                        hand_depth[e, span(row), piece(j)] = value
-                    rows[0, e, j, span(t), :] = value + bed_rows[j, span(t), :]
-                level = jnp.where(
-                    near, level_of(levels[2], dr, at), level_of(levels[0], dr, at + block_cols - 1)
-                )
-                value = SCALE * jnp.maximum(level - side_height, 0.0) + bed_rows[cols, span(t), :]
-                rows[0, e, cols, span(t), :] = jnp.where(lane_ok, value, 0.0)
-
         def one_step(base, tiles, chosen):
             end = tiles - 1
             for e in chosen:

time: 25.2 us -> 24.5 us (0.972)
  Pallas kernels: 23.5 us -> 22.8 us
    pallas_call x1, Pallas kernels: 23.5 us -> 22.8 us  [body(): pl.pallas_call(functools.partial(flood_kernel, row_total, col_total, core...]
where the time goes in v4:
time: 24.5 us; the launch traced here: 24.3 us
  Pallas kernels  22.8 us (93%)
  other arithmetic  0.84 us (3%)
  between operations  0.64 us (3%)
    pallas_call x1, Pallas kernels, body(): pl.pallas_call(functools.partial(flood_kernel, row_total, col_total, core...  22.8 us
    mul x1, other arithmetic, body(): return (start * (1.0 / SCALE), end * (1.0 / SCALE))  0.84 us

profile of v4, /device:TPU:17, one launch (start us, length us, event | category | flops | bytes accessed | tf_op | source)
XLA Modules:
  0.0 24.3 jit_solution(14793103586355654062)
XLA Ops:
  0.6 22.8 %flood.1 = (f32[2,32,1024]{2,1,0:T(8,128)S(1)}, f32[2,32,1024]{2,1,0:T(8,128)S(1)}) custom-call(f32[2,256]{1,0:T(2,128)} %sections_in.1, s32[1,1,4,64]{3,2,1,0:T(4,128)} %send_list_in.1, s32[1,1,4]{2,1,0:T(1,128)} %send_count_in.1, s32[1,1,32]{2,1,0:T(1,128)} %slot_position_in.1, s32[4,8]{1,0:T(4,128)} %block_slot_in.1, f32[32,1024]{1,0:T(8,128)} %hand.1, ...), custom_call_target="tpu_custom_call" | custom-call | tf_op jit(solution)/shard_map/flood/pallas_call | solution.py:641
  23.4 0.8 %broadcast_multiply_fusion = (f32[2,32,1024]{2,1,0:T(8,128)}, f32[2,32,1024]{2,1,0:T(8,128)}) fusion(f32[2,32,1024]{2,1,0:T(8,128)S(1)} %get-tuple-element.5, f32[2,32,1024]{2,1,0:T(8,128)S(1)} %get-tuple-element.4), kind=kLoop, calls=%fused_computation | loop fusion | flops 131072 | bytes 1048576 | tf_op jit(solution)/shard_map/mul | solution.py:682

commit v5 on v4

--- a/solution.py
+++ b/solution.py
@@ -28,7 +28,7 @@
 EDGE_STEPS = ((6, 7), (5, 9))
 INNER_STEPS = ((8, 3), (7, 4), (6, 4), (5, 5))
 
-TOGETHER_TILES = 6
+TOGETHER_TILES = 5
 
 
 def phases(has_north, has_south, own_tiles):
@@ -216,9 +216,6 @@
                     for array in range(3):
                         strip_copy(index, array, dr, dc).start()
 
-    @pl.when(r < row_total - 1)
-    def _():
-        send_strips(earlier)
 
     lane = lax.broadcasted_iota(jnp.int32, (SUBLANES, LANES), 1)
     row_id = lax.broadcasted_iota(jnp.int32, (SUBLANES, LANES), 0)
@@ -305,9 +302,7 @@
 
     send_place(earlier)
 
-    @pl.when(r == row_total - 1)
-    def _():
-        send_strips(earlier)
+    send_strips(earlier)
 
     behind = sum(as_int(tile_exists(dr, dc)) for dr, dc in later)
 
@@ -316,8 +311,8 @@
         pl.semaphore_wait(near_sem, behind)
 
     send_levels(lambda rr, dc: jnp.logical_and(is_later(rr, dc), is_near(rr, dc)))
+    send_place(later)
     send_strips(later)
-    send_place(later)
     reach = sum(as_int(col_exists(dc)) for dc in (-1, 0, 1))
     for row in range(row_total):
         @pl.when(row > r + 1)

time: 24.5 us -> 24.2 us (0.988)
  no operation moved by 1% of the time
where the time goes in v5:
time: 24.2 us; the launch traced here: 24.1 us
  Pallas kernels  22.6 us (93%)
  other arithmetic  0.84 us (3%)
  between operations  0.64 us (3%)
    pallas_call x1, Pallas kernels, body(): pl.pallas_call(functools.partial(flood_kernel, row_total, col_total, core...  22.6 us
    mul x1, other arithmetic, body(): return (start * (1.0 / SCALE), end * (1.0 / SCALE))  0.84 us

profile of v5, /device:TPU:17, one launch (start us, length us, event | category | flops | bytes accessed | tf_op | source)
XLA Modules:
  0.0 24.1 jit_solution(2122380689108321535)
XLA Ops:
  0.6 22.6 %flood.1 = (f32[2,32,1024]{2,1,0:T(8,128)S(1)}, f32[2,32,1024]{2,1,0:T(8,128)S(1)}) custom-call(f32[2,256]{1,0:T(2,128)} %sections_in.1, s32[1,1,4,64]{3,2,1,0:T(4,128)} %send_list_in.1, s32[1,1,4]{2,1,0:T(1,128)} %send_count_in.1, s32[1,1,32]{2,1,0:T(1,128)} %slot_position_in.1, s32[4,8]{1,0:T(4,128)} %block_slot_in.1, f32[32,1024]{1,0:T(8,128)} %hand.1, ...), custom_call_target="tpu_custom_call" | custom-call | tf_op jit(solution)/shard_map/flood/pallas_call | solution.py:636
  23.2 0.8 %broadcast_multiply_fusion = (f32[2,32,1024]{2,1,0:T(8,128)}, f32[2,32,1024]{2,1,0:T(8,128)}) fusion(f32[2,32,1024]{2,1,0:T(8,128)S(1)} %get-tuple-element.5, f32[2,32,1024]{2,1,0:T(8,128)S(1)} %get-tuple-element.4), kind=kLoop, calls=%fused_computation | loop fusion | flops 131072 | bytes 1048576 | tf_op jit(solution)/shard_map/mul | solution.py:677
